TPU v7x, 128 devices: a whole 4x4x4 slice. The times are simulated.
128 devices in a mesh: frame: 8 (over x, core), cell: 16 (over y, z).
Axes of the slice: x: 4, y: 4, z: 4, core: 2. Of those that a mesh axis runs over, the one named last changes fastest.
Arguments:
- front: float32 [8, 4096, 4096], P('frame', 'cell')
- parent_of: int32 [8], replicated, may hold values from 0 to 7
- block_map: int32 [8, 13], replicated, may hold values from 3 to 31, as said below
- parent_in: bfloat16 [8, 2, 4096, 8192], P('frame', None, 'cell'), may hold values from -0.3125 to 0.3125
Outputs:
- lower_panel: float32 [8, 4096, 768], P('frame', 'cell')
- parent_out: bfloat16 [8, 2, 4096, 8192], P('frame', None, 'cell')
Inputs may be any that keep to these rules, and one draw needn't show every extreme that they name: block_map[c, k] is 3 + k or 3 + k + 16.
All inputs are finite; a program needn't handle non-finite values.
Results may differ from a plain program's by a relative error of at most 0.004.
Values may be sent and summed in bfloat16 or wider, within the bound.
A program may use at most 192 MiB of HBM per device.

v0:
```python
import jax
import jax.numpy as jnp
from jax import lax
from jax.sharding import PartitionSpec as P

PB = 3


def per_device(front, parent_of, block_map, parent_in):
    block_row = front[0]
    rows_here = block_row.shape[0]
    order = block_row.shape[1]
    blocks = order // rows_here
    width = PB * rows_here
    cell_index = lax.axis_index("cell")
    frame_index = lax.axis_index("frame")
    highest = lax.Precision.HIGHEST
    panel = lax.all_gather(block_row[:, :width], "cell", axis=0, tiled=True)
    l11 = jnp.linalg.cholesky(panel[:width])
    l21 = lax.linalg.triangular_solve(
        l11, panel[width:], left_side=False, lower=True, transpose_a=True
    )
    lower_all = jnp.concatenate([l11, l21], 0)
    my_lower = lax.dynamic_slice_in_dim(lower_all, cell_index * rows_here, rows_here, 0)
    product = jnp.dot(my_lower, l21.T, precision=highest)
    update = (block_row[:, width:] - product).astype(jnp.bfloat16)
    update_blocks = update.shape[1] // rows_here
    which_k = jnp.maximum(cell_index - PB, 0)
    whole_parent = parent_in[0].reshape(2, rows_here, 2, blocks, rows_here)
    region_start = whole_parent[:, :, :, PB:, :].astype(jnp.float32)
    pieces = lax.all_gather(update[None], "frame", axis=0, tiled=True)

    def one_child(step, acc):
        parent = lax.dynamic_index_in_dim(parent_of, step, 0, keepdims=False)
        positions = lax.dynamic_index_in_dim(block_map, step, 0, keepdims=False)
        target = lax.dynamic_index_in_dim(positions, which_k, 0, keepdims=False)
        live = (parent == frame_index) & (cell_index >= PB)
        half = target // blocks

        def add_piece(inner):
            piece = lax.dynamic_index_in_dim(pieces, step, 0, keepdims=False)
            piece = piece.reshape(rows_here, update_blocks, rows_here).astype(jnp.float32)
            upper = (positions >= blocks)[None, :, None]
            zeros = jnp.zeros_like(piece)
            delta = jnp.stack([jnp.where(upper, zeros, piece), jnp.where(upper, piece, zeros)], 1)
            current = lax.dynamic_index_in_dim(inner, half, 0, keepdims=False)
            return lax.dynamic_update_index_in_dim(inner, current + delta, half, 0)

        def keep_same(inner):
            return inner

        return lax.cond(live, add_piece, keep_same, acc)

    total = lax.fori_loop(0, pieces.shape[0], one_child, region_start)
    merged = jnp.concatenate([whole_parent[:, :, :, :PB, :], total.astype(jnp.bfloat16)], 3)
    merged = merged.reshape(2, rows_here, 2 * blocks * rows_here)
    return (my_lower[None], merged[None])


def solution(mesh):
    placed = (P("frame", "cell", None), P(), P(), P("frame", None, "cell", None))
    return jax.shard_map(
        per_device,
        mesh=mesh,
        in_specs=placed,
        out_specs=(P("frame", "cell", None), P("frame", None, "cell", None)),
        check_vma=False,
    )
```

profile of v0, /device:TPU:15, one launch (start us, length us, event | category | flops | bytes accessed | tf_op | source)
XLA Modules:
  0.0 594.5 jit_solution(12432647070224209038)
XLA Ops:
  7.2 5.6 copy.11
  15.0 101.0 %all-gather.4.cloned.1.call-done = f32[4096,768]{0,1:T(8,128)} async-done(((f32[256,768]{0,1:T(8,128)}), f32[4096,768]{0,1:T(8,128)}) %all-gather.4.cloned.1.call-update) | async-done | bytes 12582928 | tf_op jit(solution)/shard_map/all_gather | solution.py:18
  119.6 2.7 fusion.25
  123.7 11.7 %cholesky.165 = f32[128,128]{1,0:T(8,128)S(1)} custom-call(f32[128,128]{1,0:T(8,128)S(1)} %cholesky.424), custom_call_target="Cholesky" | custom-call | tf_op jit(solution)/shard_map/jit(cholesky)/cholesky | solution.py:19
  135.4 9.8 %custom-call.46 = f32[1,128,128]{1,2,0:T(8,128)S(1)} custom-call(f32[1,128,128]{2,1,0:T(8,128)S(1)} %get-tuple-element.497), custom_call_target="InvertDiagBlocksLowerTriangular" | custom-call | tf_op jit(solution)/shard_map/jit(cholesky)/cholesky | solution.py:19
  148.2 11.7 %cholesky.188 = f32[128,128]{1,0:T(8,128)S(1)} custom-call(f32[128,128]{1,0:T(8,128)S(1)} %cholesky.428), custom_call_target="Cholesky" | custom-call | tf_op jit(solution)/shard_map/jit(cholesky)/cholesky | solution.py:19
  160.0 10.1 %custom-call.47 = f32[1,128,128]{1,2,0:T(8,128)S(1)} custom-call(f32[1,128,128]{2,1,0:T(8,128)S(1)} %get-tuple-element.494), custom_call_target="InvertDiagBlocksLowerTriangular" | custom-call | tf_op jit(solution)/shard_map/jit(cholesky)/cholesky | solution.py:19
  172.0 11.7 %cholesky.354 = f32[128,128]{1,0:T(8,128)S(1)} custom-call(f32[128,128]{1,0:T(8,128)S(1)} %cholesky.433), custom_call_target="Cholesky" | custom-call | tf_op jit(solution)/shard_map/jit(cholesky)/cholesky | solution.py:19
  184.4 9.8 %custom-call.48 = f32[1,128,128]{1,2,0:T(8,128)S(1)} custom-call(f32[1,128,128]{2,1,0:T(8,128)S(1)} %get-tuple-element.491), custom_call_target="InvertDiagBlocksLowerTriangular" | custom-call | tf_op jit(solution)/shard_map/jit(cholesky)/cholesky | solution.py:19
  196.1 11.9 %cholesky.373 = f32[128,128]{1,0:T(8,128)S(1)} custom-call(f32[128,128]{1,0:T(8,128)S(1)} %cholesky.438), custom_call_target="Cholesky" | custom-call | tf_op jit(solution)/shard_map/jit(cholesky)/cholesky | solution.py:19
  208.7 9.8 %custom-call.49 = f32[1,128,128]{1,2,0:T(8,128)S(1)} custom-call(f32[1,128,128]{2,1,0:T(8,128)S(1)} %get-tuple-element.488), custom_call_target="InvertDiagBlocksLowerTriangular" | custom-call | tf_op jit(solution)/shard_map/jit(cholesky)/cholesky | solution.py:19
  220.3 11.7 %cholesky.392 = f32[128,128]{1,0:T(8,128)S(1)} custom-call(f32[128,128]{1,0:T(8,128)S(1)} %cholesky.443), custom_call_target="Cholesky" | custom-call | tf_op jit(solution)/shard_map/jit(cholesky)/cholesky | solution.py:19
  232.7 9.8 %custom-call.50 = f32[1,128,128]{1,2,0:T(8,128)S(1)} custom-call(f32[1,128,128]{2,1,0:T(8,128)S(1)} %get-tuple-element.485), custom_call_target="InvertDiagBlocksLowerTriangular" | custom-call | tf_op jit(solution)/shard_map/jit(cholesky)/cholesky | solution.py:19
  244.0 12.1 %cholesky.410 = f32[128,128]{1,0:T(8,128)S(1)} custom-call(f32[128,128]{1,0:T(8,128)S(1)} %convolution_subtract_fusion.8), custom_call_target="Cholesky" | custom-call | tf_op jit(solution)/shard_map/jit(cholesky)/cholesky | solution.py:19
  261.1 2.5 fusion.26
  263.5 17.4 %while.21 = (s32[]{:T(128)}, f32[768,768]{1,0:T(8,128)}, s32[6,2]{0,1:T(2,128)S(1)}, f32[6,128,128]{2,1,0:T(8,128)S(1)}, s32[]{:T(128)}) while((s32[]{:T(128)}, f32[768,768]{1,0:T(8,128)}, s32[6,2]{0,1:T(2,128)S(1)}, f32[6,128,128]{2,1,0:T(8,128)S(1)}, s32[]{:T(128)}) %tuple.115), condition=%wide.while_cond, body=%wide.while_body.sunk | while | flops 2 | bytes 131181 | solution.py:20
  264.2 2.3 bitcast_dynamic-update-slice_fusion.2
  267.1 2.3 bitcast_dynamic-update-slice_fusion.2
  270.0 2.3 bitcast_dynamic-update-slice_fusion.2
  272.9 2.3 bitcast_dynamic-update-slice_fusion.2
  275.8 2.3 bitcast_dynamic-update-slice_fusion.2
  281.0 59.0 %custom-call.51 = f32[6,128,128]{1,2,0:T(8,128)S(1)} custom-call(f32[6,128,128]{2,1,0:T(8,128)S(1)} %get-tuple-element.425), custom_call_target="InvertDiagBlocksLowerTriangular" | custom-call | tf_op jit(solution)/shard_map/triangular_solve | solution.py:20
  342.1 3.1 constant_dynamic-update-slice_fusion.4
  345.2 3.3 convolution_subtract_fusion.3
  350.3 3.8 convolution_subtract_fusion.2
  354.0 2.6 constant_dynamic-update-slice_fusion.2
  356.6 3.2 copy-done.1
  359.9 4.9 fusion.16
  364.8 4.3 constant_dynamic-update-slice_fusion.1
  369.2 7.1 %fusion.19 = f32[3328,128]{0,1:T(8,128)} fusion(f32[3328,128]{0,1:T(8,128)} %get-tuple-element.503, f32[3328,128]{0,1:T(8,128)} %copy-done.2, f32[3328,128]{0,1:T(8,128)S(1)} %get-tuple-element.501, f32[3328,128]{0,1:T(8,128)S(1)} %bitcast.107, f32[4096,768]{0,1:T(8,128)S(1)} %bitcast.111, f32[768,768]{1,0:T(8,128)} %get-tuple-element.639), kind=kOutput, calls=%fused_computation.35 | convolution fusion | flops 2622783488 | bytes 10485760 | tf_op jit(solution)/shard_map/triangular_solve | solution.py:20
  376.3 4.3 constant_dynamic-update-slice_fusion
  380.6 8.5 %convolution_subtract_fusion.1 = f32[3328,128]{0,1:T(8,128)S(1)} fusion(f32[3328,640]{0,1:T(8,128)} %get-tuple-element.472, f32[4096,768]{0,1:T(8,128)S(1)} %bitcast.111, f32[768,768]{1,0:T(8,128)} %get-tuple-element.639), kind=kOutput, calls=%fused_computation.31 | convolution fusion | flops 3271983104 | bytes 12255232 | tf_op jit(solution)/shard_map/triangular_solve | solution.py:20
  389.1 2.5 convolution_dynamic-update-slice_fusion
  393.8 18.2 %fusion.9 = bf16[256,3328]{0,1:T(8,128)(2,1)} fusion(f32[256,768]{0,1:T(8,128)S(1)} %fusion.29, f32[3328,768]{0,1:T(8,128)S(1)} %convolution_dynamic-update-slice_fusion, f32[256,4096]{0,1:T(8,128)S(1)} %bitcast.109), kind=kOutput, calls=%fused_computation.24 | convolution fusion | flops 7853441024 | bytes 16121856 | tf_op jit(solution)/shard_map/dot_general | solution.py:25
  412.0 12.0 %copy.15 = bf16[1,2,256,8192]{2,3,1,0:T(8,128)(2,1)} copy(bf16[1,2,256,8192]{3,2,1,0:T(8,128)(2,1)} %param.11) | data formatting | bytes 16777216 | tf_op args[3]
  425.7 9.8 %slice_convert_fusion = f32[2,256,2,13,256]{1,4,3,2,0:T(8,128)} fusion(bf16[2,256,2,16,256]{1,4,3,2,0:T(8,128)(2,1)} %bitcast.103), kind=kLoop, calls=%fused_computation.13 | loop fusion | flops 3407872 | bytes 20447232 | tf_op jit(solution)/shard_map/convert_element_type | solution.py:30
  436.7 52.1 %all-gather.6.cloned.1.call-done = bf16[2048,3328]{0,1:T(8,128)(2,1)} async-done(((bf16[256,3328]{0,1:T(8,128)(2,1)}), bf16[2048,3328]{0,1:T(8,128)(2,1)}) %all-gather.6.cloned.1.call-update) | async-done | bytes 13631504 | tf_op jit(solution)/shard_map/all_gather | solution.py:31
  488.8 12.5 %copy.23 = bf16[416,8,8,256]{3,2,0,1:T(8,128)(2,1)} copy(bf16[416,8,8,256]{3,2,1,0:T(8,128)(2,1)} %bitcast.112) | data formatting | bytes 27262976 | tf_op jit(solution)/shard_map/all_gather | solution.py:31
  501.3 58.4 %while.20 = (s32[]{:T(128)}, f32[2,256,2,13,256]{1,4,3,2,0:T(8,128)}, s32[8]{0:T(128)S(1)}, s32[]{:T(128)}, pred[]{:T(512)}, /*index=5*/s32[8,13]{1,0:T(8,128)},...) while((s32[]{:T(128)}, f32[2,256,2,13,256]{1,4,3,2,0:T(8,128)}, ...), condition=%wide.region_15.16_spmd, body=%wide.region_12.15_spmd.sunk | while | flops 5963816 | bytes 32375320 | solution.py:54
  504.1 12.4 %conditional.2 = (f32[2,256,2,13,256]{1,4,3,2,0:T(8,128)}) conditional(s32[]{:T(128)} %convert_element_type.50, f32[2,256,2,13,256]{1,4,3,2,0:T(8,128)} %get-tuple-element.611, (s32[]{:T(128)}, s32[]{:T(128)}, f32[2,256,2,13,256]{1,4,3,2,0:T(8,128)}, s32[8,13]{1,0:T(8,128)}, s32[]{:T(128)}, /*index=5*/bf16[8,256,3328]{1,2,0:T(8,128)(2,1)}, ...), branch_computations={%region_13.13_spmd, %region_14.14_spmd} | conditional | flops 5963810 | bytes 32375100 | solution.py:52
  509.9 6.6 %fusion = f32[2,256,2,13,256]{1,4,3,2,0:T(8,128)} fusion(f32[2,256,2,13,256]{1,4,3,2,0:T(8,128)} %get-tuple-element.397, s32[]{:T(128)S(6)} %select_n.87, f32[1,256,1,13,256]{1,4,3,2,0:T(8,128)S(1)} %get-tuple-element.469, f32[1,256,1,13,256]{1,4,3,2,0:T(8,128)S(1)} %get-tuple-element.468), kind=kLoop, calls=%fused_computation.1 | loop fusion | flops 3407872 | bytes 20447236 | tf_op jit(solution)/shard_map/while/body/eval_jaxpr/cond/branch_1_fun/jit(dynamic_update_index_in_dim)/dynamic_update_slice | solution.py:47
  527.0 12.5 %conditional.2 = (f32[2,256,2,13,256]{1,4,3,2,0:T(8,128)}) conditional(s32[]{:T(128)} %convert_element_type.50, f32[2,256,2,13,256]{1,4,3,2,0:T(8,128)} %get-tuple-element.611, (s32[]{:T(128)}, s32[]{:T(128)}, f32[2,256,2,13,256]{1,4,3,2,0:T(8,128)}, s32[8,13]{1,0:T(8,128)}, s32[]{:T(128)}, /*index=5*/bf16[8,256,3328]{1,2,0:T(8,128)(2,1)}, ...), branch_computations={%region_13.13_spmd, %region_14.14_spmd} | conditional | flops 5963810 | bytes 32375100 | solution.py:52
  532.8 6.6 %fusion = f32[2,256,2,13,256]{1,4,3,2,0:T(8,128)} fusion(f32[2,256,2,13,256]{1,4,3,2,0:T(8,128)} %get-tuple-element.397, s32[]{:T(128)S(6)} %select_n.87, f32[1,256,1,13,256]{1,4,3,2,0:T(8,128)S(1)} %get-tuple-element.469, f32[1,256,1,13,256]{1,4,3,2,0:T(8,128)S(1)} %get-tuple-element.468), kind=kLoop, calls=%fused_computation.1 | loop fusion | flops 3407872 | bytes 20447236 | tf_op jit(solution)/shard_map/while/body/eval_jaxpr/cond/branch_1_fun/jit(dynamic_update_index_in_dim)/dynamic_update_slice | solution.py:47
  542.0 12.4 %conditional.2 = (f32[2,256,2,13,256]{1,4,3,2,0:T(8,128)}) conditional(s32[]{:T(128)} %convert_element_type.50, f32[2,256,2,13,256]{1,4,3,2,0:T(8,128)} %get-tuple-element.611, (s32[]{:T(128)}, s32[]{:T(128)}, f32[2,256,2,13,256]{1,4,3,2,0:T(8,128)}, s32[8,13]{1,0:T(8,128)}, s32[]{:T(128)}, /*index=5*/bf16[8,256,3328]{1,2,0:T(8,128)(2,1)}, ...), branch_computations={%region_13.13_spmd, %region_14.14_spmd} | conditional | flops 5963810 | bytes 32375100 | solution.py:52
  547.8 6.6 %fusion = f32[2,256,2,13,256]{1,4,3,2,0:T(8,128)} fusion(f32[2,256,2,13,256]{1,4,3,2,0:T(8,128)} %get-tuple-element.397, s32[]{:T(128)S(6)} %select_n.87, f32[1,256,1,13,256]{1,4,3,2,0:T(8,128)S(1)} %get-tuple-element.469, f32[1,256,1,13,256]{1,4,3,2,0:T(8,128)S(1)} %get-tuple-element.468), kind=kLoop, calls=%fused_computation.1 | loop fusion | flops 3407872 | bytes 20447236 | tf_op jit(solution)/shard_map/while/body/eval_jaxpr/cond/branch_1_fun/jit(dynamic_update_index_in_dim)/dynamic_update_slice | solution.py:47
  559.6 8.7 %convert_element_type.45 = bf16[2,256,2,13,256]{1,4,3,2,0:T(8,128)(2,1)} convert(f32[2,256,2,13,256]{1,4,3,2,0:T(8,128)} %get-tuple-element.415) | non-fusion elementwise | flops 3407872 | bytes 20447232 | tf_op jit(solution)/shard_map/convert_element_type | solution.py:55
  568.4 6.9 %pad_maximum_fusion = bf16[2,256,2,16,256]{1,4,3,2,0:T(8,128)(2,1)} fusion(bf16[2,256,2,13,256]{1,4,3,2,0:T(8,128)(2,1)} %convert_element_type.45, bf16[2,256,2,3,256]{1,4,3,2,0:T(8,128)(2,1)S(1)} %slice.203), kind=kLoop, calls=%fused_computation.12 | loop fusion | flops 4194304 | bytes 16777216 | tf_op jit(solution)/shard_map/concatenate | solution.py:55
  575.2 12.0 %copy.20 = bf16[1,2,256,8192]{3,2,1,0:T(8,128)(2,1)} copy(bf16[1,2,256,8192]{2,3,1,0:T(8,128)(2,1)} %bitcast.104) | data formatting | bytes 16777216 | tf_op jit(solution)/shard_map/broadcast_in_dim;reshape | solution.py:57
  (104 shorter events, 60.4 us)
Async XLA Ops:
  7.2 108.8 %all-gather.4.cloned.1.call-start = ((), (), s32[]{:S(2)}) async-start(), calls=%async_computation | async-start | bytes 13369344 | tf_op jit(solution)/shard_map/all_gather | solution.py:18
  14.9 473.9 %all-gather.6.cloned.1.call-start = ((), (), s32[]{:S(2)}) async-start(), calls=%async_computation.1 | async-start | bytes 15335424 | tf_op jit(solution)/shard_map/all_gather | solution.py:31
  115.9 1.7 slice-start.3
  122.3 1.4 copy-start.3
  339.9 8.6 %copy-start.4 = (f32[6,128,128]{1,2,0:T(8,128)}, f32[6,128,128]{1,2,0:T(8,128)S(1)}, u32[]{:S(2)}) copy-start(f32[6,128,128]{1,2,0:T(8,128)S(1)} %custom-call.51) | copy-start | bytes 1179652
  345.2 14.6 %slice-start = ((s8[12582912]{0:T(1024)(128)(4,1)}), s8[4194304]{0:T(1024)(128)(4,1)S(1)}, s32[]{:S(2)}) async-start(s8[12582912]{0:T(1024)(128)(4,1)} %bitcast.110), calls=%async_computation.2 | async-start | bytes 8388608
  348.5 11.3 %slice-start.1 = ((s8[12582912]{0:T(1024)(128)(4,1)}), s8[4194304]{0:T(1024)(128)(4,1)S(1)}, s32[]{:S(2)}) async-start(s8[12582912]{0:T(1024)(128)(4,1)} %bitcast.110), calls=%async_computation.3 | async-start | bytes 8388608
  350.3 9.6 %slice-start.2 = ((s8[12582912]{0:T(1024)(128)(4,1)}), s8[4194304]{0:T(1024)(128)(4,1)S(1)}, s32[]{:S(2)}) async-start(s8[12582912]{0:T(1024)(128)(4,1)} %bitcast.110), calls=%async_computation.4 | async-start | bytes 8388608
  356.6 3.2 copy-start.1
  359.9 5.0 copy-start.2
  391.6 2.2 copy-start
  488.8 12.5 %copy-start.5 = (s32[8]{0:T(128)S(1)}, s32[8]{0:T(128)}, u32[]{:S(2)}) copy-start(s32[8]{0:T(128)} %param.9) | copy-start | bytes 100
Sparse Core Ops, SparseCore 0:
  15.0 100.8 all-gather.3
  412.1 76.6 all-gather.5
where the time goes:
time: 606 us; the launch traced here: 594 us
  other arithmetic  238 us (39%)
  waiting for transfers between devices  153 us (25%)
  local copies, waits for them, and re-layouts  97.1 us (16%)
  matrix products  74 us (12%)
  between operations  18.5 us (3%)
  loops' own time  14 us (2%)
    another operation x22, other arithmetic, per_device(): l11 = jnp.linalg.cholesky(panel[:width])  124 us
    all_gather x1, waiting for transfers between devices, per_device(): panel = lax.all_gather(block_row[:, :width], 'cell', axis=0, tiled=True)  101 us
    another operation x3, other arithmetic, per_device(): lax.linalg.triangular_solve(l11, panel[width:], left_side=False, lower=Tr...  61.4 us
    all_gather x1, waiting for transfers between devices, per_device(): pieces = lax.all_gather(update[None], 'frame', axis=0, tiled=True)  52.1 us
    another operation x11, matrix products, per_device(): lax.linalg.triangular_solve(l11, panel[width:], left_side=False, lower=Tr...  46.1 us
    unnamed x20, local copies, waits for them, and re-layouts  24.3 us
    dynamic_update_slice x3, other arithmetic, add_piece(): return lax.dynamic_update_index_in_dim(inner, current + delta, half, 0)  19.8 us
    dot_general x1, matrix products, per_device(): product = jnp.dot(my_lower, l21.T, precision=highest)  18.2 us
  transfers between devices with their start and end apart: 2, of which 2 were waited for; matrix products, arithmetic and copies ran while one was open for 4% of the time, Pallas kernels for 0%

commit v1 on v0

--- a/solution.py
+++ b/solution.py
@@ -28,7 +28,9 @@
     which_k = jnp.maximum(cell_index - PB, 0)
     whole_parent = parent_in[0].reshape(2, rows_here, 2, blocks, rows_here)
     region_start = whole_parent[:, :, :, PB:, :].astype(jnp.float32)
-    pieces = lax.all_gather(update[None], "frame", axis=0, tiled=True)
+    pieces = jnp.concatenate(
+        lax.all_to_all(jnp.stack([update[None]] * lax.axis_size("frame")), "frame", 0, 0), axis=0
+    )
 
     def one_child(step, acc):
         parent = lax.dynamic_index_in_dim(parent_of, step, 0, keepdims=False)

time: 606 us -> 676 us (1.12)
  waiting for transfers between devices: 153 us -> 225 us
  starting transfers between devices: 0.08 us -> 7.47 us
  local copies, waits for them, and re-layouts: 97.1 us -> 90 us
    all_to_all x0 -> x1, waiting for transfers between devices: none -> 124 us  [per_device(): lax.all_to_all(jnp.stack([update[None]] * lax.axis_size('frame')), 'frame...]
    all_gather x1 -> x0, waiting for transfers between devices: 52.1 us -> none  [per_device(): pieces = lax.all_gather(update[None], 'frame', axis=0, tiled=True)]
    all_gather x1 -> x0, local copies, waits for them, and re-layouts: 12.5 us -> none  [per_device(): pieces = lax.all_gather(update[None], 'frame', axis=0, tiled=True)]
    all_to_all x0 -> x1, starting transfers between devices: none -> 7.43 us  [per_device(): lax.all_to_all(jnp.stack([update[None]] * lax.axis_size('frame')), 'frame...]
    another operation x18 -> x19, local copies, waits for them, and re-layouts: 17.3 us -> 23.8 us
where the time goes in v1:
time: 676 us; the launch traced here: 664 us
  other arithmetic  238 us (35%)
  waiting for transfers between devices  225 us (33%)
  local copies, waits for them, and re-layouts  90 us (13%)
  matrix products  73.4 us (11%)
  between operations  18.7 us (3%)
  loops' own time  12.2 us (2%)
  starting transfers between devices  7.47 us (1%)
    all_to_all x1, waiting for transfers between devices, per_device(): lax.all_to_all(jnp.stack([update[None]] * lax.axis_size('frame')), 'frame...  124 us
    another operation x22, other arithmetic, per_device(): l11 = jnp.linalg.cholesky(panel[:width])  124 us
    all_gather x1, waiting for transfers between devices, per_device(): panel = lax.all_gather(block_row[:, :width], 'cell', axis=0, tiled=True)  101 us
    another operation x3, other arithmetic, per_device(): lax.linalg.triangular_solve(l11, panel[width:], left_side=False, lower=Tr...  61.4 us
    another operation x11, matrix products, per_device(): lax.linalg.triangular_solve(l11, panel[width:], left_side=False, lower=Tr...  46.1 us
    unnamed x20, local copies, waits for them, and re-layouts  24.2 us
    dynamic_update_slice x3, other arithmetic, add_piece(): return lax.dynamic_update_index_in_dim(inner, current + delta, half, 0)  19.8 us
    another operation x18, local copies, waits for them, and re-layouts  18 us
  transfers between devices with their start and end apart: 2, of which 2 were waited for; matrix products, arithmetic and copies ran while one was open for 4% of the time, Pallas kernels for 0%

profile of v1, /device:TPU:15, one launch (start us, length us, event | category | flops | bytes accessed | tf_op | source)
XLA Modules:
  0.0 664.4 jit_solution(3741607135633893238)
XLA Ops:
  7.2 5.6 copy.18
  14.9 101.0 %all-gather.2.cloned.1.call-done = f32[4096,768]{0,1:T(8,128)} async-done(((f32[256,768]{0,1:T(8,128)}), f32[4096,768]{0,1:T(8,128)}) %all-gather.2.cloned.1.call-update) | async-done | bytes 12582928 | tf_op jit(solution)/shard_map/all_gather | solution.py:18
  119.6 2.7 fusion.25
  123.7 11.7 %cholesky.165 = f32[128,128]{1,0:T(8,128)S(1)} custom-call(f32[128,128]{1,0:T(8,128)S(1)} %cholesky.424), custom_call_target="Cholesky" | custom-call | tf_op jit(solution)/shard_map/jit(cholesky)/cholesky | solution.py:19
  135.4 9.8 %custom-call.46 = f32[1,128,128]{1,2,0:T(8,128)S(1)} custom-call(f32[1,128,128]{2,1,0:T(8,128)S(1)} %get-tuple-element.481), custom_call_target="InvertDiagBlocksLowerTriangular" | custom-call | tf_op jit(solution)/shard_map/jit(cholesky)/cholesky | solution.py:19
  148.2 11.7 %cholesky.188 = f32[128,128]{1,0:T(8,128)S(1)} custom-call(f32[128,128]{1,0:T(8,128)S(1)} %cholesky.428), custom_call_target="Cholesky" | custom-call | tf_op jit(solution)/shard_map/jit(cholesky)/cholesky | solution.py:19
  160.0 10.1 %custom-call.47 = f32[1,128,128]{1,2,0:T(8,128)S(1)} custom-call(f32[1,128,128]{2,1,0:T(8,128)S(1)} %get-tuple-element.478), custom_call_target="InvertDiagBlocksLowerTriangular" | custom-call | tf_op jit(solution)/shard_map/jit(cholesky)/cholesky | solution.py:19
  172.0 11.7 %cholesky.354 = f32[128,128]{1,0:T(8,128)S(1)} custom-call(f32[128,128]{1,0:T(8,128)S(1)} %cholesky.433), custom_call_target="Cholesky" | custom-call | tf_op jit(solution)/shard_map/jit(cholesky)/cholesky | solution.py:19
  184.5 9.8 %custom-call.48 = f32[1,128,128]{1,2,0:T(8,128)S(1)} custom-call(f32[1,128,128]{2,1,0:T(8,128)S(1)} %get-tuple-element.475), custom_call_target="InvertDiagBlocksLowerTriangular" | custom-call | tf_op jit(solution)/shard_map/jit(cholesky)/cholesky | solution.py:19
  196.2 11.9 %cholesky.373 = f32[128,128]{1,0:T(8,128)S(1)} custom-call(f32[128,128]{1,0:T(8,128)S(1)} %cholesky.438), custom_call_target="Cholesky" | custom-call | tf_op jit(solution)/shard_map/jit(cholesky)/cholesky | solution.py:19
  208.8 9.8 %custom-call.49 = f32[1,128,128]{1,2,0:T(8,128)S(1)} custom-call(f32[1,128,128]{2,1,0:T(8,128)S(1)} %get-tuple-element.472), custom_call_target="InvertDiagBlocksLowerTriangular" | custom-call | tf_op jit(solution)/shard_map/jit(cholesky)/cholesky | solution.py:19
  220.4 11.7 %cholesky.392 = f32[128,128]{1,0:T(8,128)S(1)} custom-call(f32[128,128]{1,0:T(8,128)S(1)} %cholesky.443), custom_call_target="Cholesky" | custom-call | tf_op jit(solution)/shard_map/jit(cholesky)/cholesky | solution.py:19
  232.7 9.8 %custom-call.50 = f32[1,128,128]{1,2,0:T(8,128)S(1)} custom-call(f32[1,128,128]{2,1,0:T(8,128)S(1)} %get-tuple-element.469), custom_call_target="InvertDiagBlocksLowerTriangular" | custom-call | tf_op jit(solution)/shard_map/jit(cholesky)/cholesky | solution.py:19
  244.1 12.1 %cholesky.410 = f32[128,128]{1,0:T(8,128)S(1)} custom-call(f32[128,128]{1,0:T(8,128)S(1)} %convolution_subtract_fusion.8), custom_call_target="Cholesky" | custom-call | tf_op jit(solution)/shard_map/jit(cholesky)/cholesky | solution.py:19
  261.3 2.5 fusion.26
  263.8 18.1 %while.21 = (s32[]{:T(128)}, f32[768,768]{1,0:T(8,128)}, s32[6,2]{0,1:T(2,128)S(1)}, f32[6,128,128]{2,1,0:T(8,128)S(1)}, s32[]{:T(128)}) while((s32[]{:T(128)}, f32[768,768]{1,0:T(8,128)}, s32[6,2]{0,1:T(2,128)S(1)}, f32[6,128,128]{2,1,0:T(8,128)S(1)}, s32[]{:T(128)}) %tuple.113), condition=%wide.while_cond, body=%wide.while_body.sunk | while | flops 2 | bytes 131181 | solution.py:20
  264.5 2.3 bitcast_dynamic-update-slice_fusion.2
  267.5 2.3 bitcast_dynamic-update-slice_fusion.2
  270.5 2.3 bitcast_dynamic-update-slice_fusion.2
  273.6 2.3 bitcast_dynamic-update-slice_fusion.2
  281.9 59.0 %custom-call.51 = f32[6,128,128]{1,2,0:T(8,128)S(1)} custom-call(f32[6,128,128]{2,1,0:T(8,128)S(1)} %get-tuple-element.425), custom_call_target="InvertDiagBlocksLowerTriangular" | custom-call | tf_op jit(solution)/shard_map/triangular_solve | solution.py:20
  343.1 3.1 constant_dynamic-update-slice_fusion.4
  346.2 3.3 convolution_subtract_fusion.3
  351.2 3.8 convolution_subtract_fusion.2
  355.0 2.6 constant_dynamic-update-slice_fusion.2
  357.6 3.2 copy-done.1
  360.8 4.9 fusion.16
  365.8 4.4 constant_dynamic-update-slice_fusion.1
  370.1 7.1 %fusion.19 = f32[3328,128]{0,1:T(8,128)} fusion(f32[3328,128]{0,1:T(8,128)} %get-tuple-element.487, f32[3328,128]{0,1:T(8,128)} %copy-done.2, f32[3328,128]{0,1:T(8,128)S(1)} %get-tuple-element.485, f32[3328,128]{0,1:T(8,128)S(1)} %bitcast.103, f32[4096,768]{0,1:T(8,128)S(1)} %bitcast.107, f32[768,768]{1,0:T(8,128)} %get-tuple-element.621), kind=kOutput, calls=%fused_computation.34 | convolution fusion | flops 2622783488 | bytes 10485760 | tf_op jit(solution)/shard_map/triangular_solve | solution.py:20
  377.3 4.3 constant_dynamic-update-slice_fusion
  381.5 8.5 %convolution_subtract_fusion.1 = f32[3328,128]{0,1:T(8,128)S(1)} fusion(f32[3328,640]{0,1:T(8,128)} %get-tuple-element.456, f32[4096,768]{0,1:T(8,128)S(1)} %bitcast.107, f32[768,768]{1,0:T(8,128)} %get-tuple-element.621), kind=kOutput, calls=%fused_computation.30 | convolution fusion | flops 3271983104 | bytes 12255232 | tf_op jit(solution)/shard_map/triangular_solve | solution.py:20
  390.0 2.5 convolution_dynamic-update-slice_fusion
  394.7 17.5 %fusion.9 = bf16[256,3328]{0,1:T(8,128)(2,1)S(1)} fusion(f32[256,768]{0,1:T(8,128)S(1)} %fusion.29, f32[3328,768]{0,1:T(8,128)S(1)} %convolution_dynamic-update-slice_fusion, f32[256,4096]{0,1:T(8,128)S(1)} %bitcast.105), kind=kOutput, calls=%fused_computation.23 | convolution fusion | flops 7853441024 | bytes 16121856 | tf_op jit(solution)/shard_map/dot_general | solution.py:25
  412.2 5.8 stack.8
  418.0 7.4 %all-to-all-start = ((bf16[8,1,256,3328]{2,3,1,0:T(8,128)(2,1)}), bf16[8,1,256,3328]{2,3,1,0:T(8,128)(2,1)}, u32[]{:S(2)}, u32[]{:S(2)}) async-start(bf16[8,1,256,3328]{2,3,1,0:T(8,128)(2,1)} %stack.8), calls=%async_computation | async-start | bytes 27262976 | tf_op jit(solution)/shard_map/all_to_all | solution.py:32
  425.5 11.9 %copy.27 = bf16[1,2,256,8192]{2,3,1,0:T(8,128)(2,1)} copy(bf16[1,2,256,8192]{3,2,1,0:T(8,128)(2,1)} %param.11) | data formatting | bytes 16777216 | tf_op args[3]
  438.9 9.5 %slice_convert_fusion = f32[2,256,2,13,256]{1,4,3,2,0:T(8,128)} fusion(bf16[2,256,2,16,256]{1,4,3,2,0:T(8,128)(2,1)} %bitcast.99), kind=kLoop, calls=%fused_computation.12 | loop fusion | flops 3407872 | bytes 20447232 | tf_op jit(solution)/shard_map/convert_element_type | solution.py:30
  449.6 124.1 %all-to-all-done = bf16[8,1,256,3328]{2,3,1,0:T(8,128)(2,1)} async-done(((bf16[8,1,256,3328]{2,3,1,0:T(8,128)(2,1)}), bf16[8,1,256,3328]{2,3,1,0:T(8,128)(2,1)}, u32[]{:S(2)}, u32[]{:S(2)}) %all-to-all-start) | async-done | bytes 13631520 | tf_op jit(solution)/shard_map/all_to_all | solution.py:32
  573.7 55.8 %while.20 = (s32[]{:T(128)}, f32[2,256,2,13,256]{1,4,3,2,0:T(8,128)}, s32[8]{0:T(128)S(1)}, s32[]{:T(128)}, pred[]{:T(512)}, /*index=5*/s32[8,13]{1,0:T(8,128)},...) while((s32[]{:T(128)}, f32[2,256,2,13,256]{1,4,3,2,0:T(8,128)}, ...), condition=%wide.region_15.16_spmd, body=%wide.region_12.15_spmd.sunk | while | flops 5963816 | bytes 32375320 | solution.py:56
  576.2 11.9 %conditional.2 = (f32[2,256,2,13,256]{1,4,3,2,0:T(8,128)}) conditional(s32[]{:T(128)} %convert_element_type.50, f32[2,256,2,13,256]{1,4,3,2,0:T(8,128)} %get-tuple-element.595, (s32[]{:T(128)}, s32[]{:T(128)}, f32[2,256,2,13,256]{1,4,3,2,0:T(8,128)}, s32[8,13]{1,0:T(8,128)}, s32[]{:T(128)}, /*index=5*/bf16[8,256,3328]{1,2,0:T(8,128)(2,1)}, ...), branch_computations={%region_13.13_spmd, %region_14.14_spmd} | conditional | flops 5963810 | bytes 32375100 | solution.py:54
  581.5 6.6 fusion
  598.2 11.9 %conditional.2 = (f32[2,256,2,13,256]{1,4,3,2,0:T(8,128)}) conditional(s32[]{:T(128)} %convert_element_type.50, f32[2,256,2,13,256]{1,4,3,2,0:T(8,128)} %get-tuple-element.595, (s32[]{:T(128)}, s32[]{:T(128)}, f32[2,256,2,13,256]{1,4,3,2,0:T(8,128)}, s32[8,13]{1,0:T(8,128)}, s32[]{:T(128)}, /*index=5*/bf16[8,256,3328]{1,2,0:T(8,128)(2,1)}, ...), branch_computations={%region_13.13_spmd, %region_14.14_spmd} | conditional | flops 5963810 | bytes 32375100 | solution.py:54
  603.5 6.6 fusion
  612.6 11.9 %conditional.2 = (f32[2,256,2,13,256]{1,4,3,2,0:T(8,128)}) conditional(s32[]{:T(128)} %convert_element_type.50, f32[2,256,2,13,256]{1,4,3,2,0:T(8,128)} %get-tuple-element.595, (s32[]{:T(128)}, s32[]{:T(128)}, f32[2,256,2,13,256]{1,4,3,2,0:T(8,128)}, s32[8,13]{1,0:T(8,128)}, s32[]{:T(128)}, /*index=5*/bf16[8,256,3328]{1,2,0:T(8,128)(2,1)}, ...), branch_computations={%region_13.13_spmd, %region_14.14_spmd} | conditional | flops 5963810 | bytes 32375100 | solution.py:54
  617.9 6.6 fusion
  629.6 8.7 %convert_element_type.45 = bf16[2,256,2,13,256]{1,4,3,2,0:T(8,128)(2,1)} convert(f32[2,256,2,13,256]{1,4,3,2,0:T(8,128)} %get-tuple-element.415) | non-fusion elementwise | flops 3407872 | bytes 20447232 | tf_op jit(solution)/shard_map/convert_element_type | solution.py:57
  638.3 6.9 %pad_maximum_fusion = bf16[2,256,2,16,256]{1,4,3,2,0:T(8,128)(2,1)} fusion(bf16[2,256,2,13,256]{1,4,3,2,0:T(8,128)(2,1)} %convert_element_type.45, bf16[2,256,2,3,256]{1,4,3,2,0:T(8,128)(2,1)S(1)} %slice.203), kind=kLoop, calls=%fused_computation.11 | loop fusion | flops 4194304 | bytes 16777216 | tf_op jit(solution)/shard_map/concatenate | solution.py:57
  645.1 12.0 %copy.36 = bf16[1,2,256,8192]{3,2,1,0:T(8,128)(2,1)} copy(bf16[1,2,256,8192]{2,3,1,0:T(8,128)(2,1)} %bitcast.100) | data formatting | bytes 16777216 | tf_op jit(solution)/shard_map/broadcast_in_dim;reshape | solution.py:59
  (103 shorter events, 62.1 us)
Async XLA Ops:
  7.2 108.8 %all-gather.2.cloned.1.call-start = ((), (), s32[]{:S(2)}) async-start(), calls=%async_computation.1 | async-start | bytes 13369344 | tf_op jit(solution)/shard_map/all_gather | solution.py:18
  115.9 1.7 slice-start.3
  122.3 1.4 copy-start.3
  340.9 8.6 %copy-start.4 = (f32[6,128,128]{1,2,0:T(8,128)}, f32[6,128,128]{1,2,0:T(8,128)S(1)}, u32[]{:S(2)}) copy-start(f32[6,128,128]{1,2,0:T(8,128)S(1)} %custom-call.51) | copy-start | bytes 1179652
  346.2 14.6 %slice-start = ((s8[12582912]{0:T(1024)(128)(4,1)}), s8[4194304]{0:T(1024)(128)(4,1)S(1)}, s32[]{:S(2)}) async-start(s8[12582912]{0:T(1024)(128)(4,1)} %bitcast.106), calls=%async_computation.2 | async-start | bytes 8388608
  349.5 11.3 %slice-start.1 = ((s8[12582912]{0:T(1024)(128)(4,1)}), s8[4194304]{0:T(1024)(128)(4,1)S(1)}, s32[]{:S(2)}) async-start(s8[12582912]{0:T(1024)(128)(4,1)} %bitcast.106), calls=%async_computation.3 | async-start | bytes 8388608
  351.2 9.6 %slice-start.2 = ((s8[12582912]{0:T(1024)(128)(4,1)}), s8[4194304]{0:T(1024)(128)(4,1)S(1)}, s32[]{:S(2)}) async-start(s8[12582912]{0:T(1024)(128)(4,1)} %bitcast.106), calls=%async_computation.4 | async-start | bytes 8388608
  357.5 3.2 copy-start.1
  360.8 5.0 copy-start.2
  392.5 2.2 copy-start
  418.0 155.7 %all-to-all-start = ((bf16[8,1,256,3328]{2,3,1,0:T(8,128)(2,1)}), bf16[8,1,256,3328]{2,3,1,0:T(8,128)(2,1)}, u32[]{:S(2)}, u32[]{:S(2)}) async-start(bf16[8,1,256,3328]{2,3,1,0:T(8,128)(2,1)} %stack.8), calls=%async_computation | async-start | bytes 27262976 | tf_op jit(solution)/shard_map/all_to_all | solution.py:32
  438.9 134.8 %copy-start.5 = (s32[8]{0:T(128)S(1)}, s32[8]{0:T(128)}, u32[]{:S(2)}) copy-start(s32[8]{0:T(128)} %param.9) | copy-start | bytes 100
Sparse Core Ops, SparseCore 0:
  15.0 100.8 all-gather.1
